TPU v7x, 32 devices: a whole 2x2x4 slice. The times are simulated.
32 devices in a mesh: row: 4 (over z), col: 8 (over y, x, core).
Axes of the slice: x: 2, y: 2, z: 4, core: 2. Of those that a mesh axis runs over, the one named last changes fastest.
Arguments:
- spectra: bfloat16 [256, 256, 512], P(('row', 'col')), may hold values from 0.05 to 20000
- sensor_ids: int32 [256, 1], P(('row', 'col')), may hold values from 0 to 31, as said below
- permutation: int32 [256], P(('row', 'col')), may hold values from 0 to 255, as said below
- w_enc1: bfloat16 [2048, 256], replicated, may hold values from -0.125 to 0.125
- w_enc2: bfloat16 [1024, 256], replicated, may hold values from -0.1875 to 0.1875
- w_dec1: bfloat16 [256, 1024], replicated, may hold values from -0.25 to 0.25
- w_dec2: bfloat16 [256, 2048], replicated, may hold values from -0.25 to 0.25
Outputs:
- grad_enc1: float32 [2048, 256], replicated
- grad_enc2: float32 [1024, 256], replicated
- grad_dec1: float32 [256, 1024], replicated
- grad_dec2: float32 [256, 2048], replicated
Inputs may be any that keep to these rules, and one draw needn't show every extreme that they name: `sensor_ids`: every sensor from 0 to 31 recorded exactly 8 windows. A permutation of all slots; the 8 windows of the ingest device with indices (a, b) go to 8 different trainers, one to each trainer whose col index c has c // 2 = a; each trainer thus receives one window from each ingest device of one row index.
All inputs are finite; a program needn't handle non-finite values.
Results may differ from a plain program's by a relative error of at most 0.004.
Values may be sent and summed in bfloat16 or wider, within the bound.
A program may use at most 192 MiB of HBM per device.

v0:
```python
import functools

import jax
import jax.numpy as jnp
from jax import lax
from jax.experimental import pallas as pl
from jax.experimental.pallas import tpu as pltpu
from jax.sharding import PartitionSpec as P

WIN_SENSOR = 8


EPS = 1e-05
MESH = pl.DeviceIdType.MESH
SEGMENTS = 3
WIDTH = 256


def enter(rows, cols, me_row, me_col):
    barrier = pltpu.get_barrier_semaphore()
    for k in range(1, cols):
        pl.semaphore_signal(
            barrier, inc=1, device_id=(me_row, lax.rem(me_col + k, cols)), device_id_type=MESH
        )
    for k in range(1, rows):
        pl.semaphore_signal(
            barrier, inc=1, device_id=(lax.rem(me_row + k, rows), me_col), device_id_type=MESH
        )
    pl.semaphore_wait(barrier, rows + cols - 2)


def send(src, dst, send_sem, recv_sem, device):
    copy = pltpu.make_async_remote_copy(
        src_ref=src,
        dst_ref=dst,
        send_sem=send_sem,
        recv_sem=recv_sem,
        device_id=device,
        device_id_type=MESH,
    )
    copy.start()
    return copy


def exchange_kernel(
    rows, cols, order_ref, spectra_ref, label_ref, table_ref,
    raw_ref, got_label_ref, stats_ref,
    sorted_buf, sums, part, part_in, share, share_in,
    raw_send, raw_recv, lab_send, lab_recv, a_send, a_recv, b_send, b_recv, c_send, c_recv,
):
    me_row, me_col = lax.axis_index("row"), lax.axis_index("col")
    windows, frames, _ = spectra_ref.shape
    step = 64
    for w in range(windows):
        sorted_buf[w] = spectra_ref[order_ref[w]]
    enter(rows, cols, me_row, me_col)
    copies = []
    for k in range(1, cols):
        peer = lax.rem(me_col + k, cols)
        device = (me_row, peer)
        copies.append(send(sorted_buf.at[peer], raw_ref.at[me_col], raw_send.at[k], raw_recv.at[k], device))
        copies.append(send(label_ref.at[peer], got_label_ref.at[me_col], lab_send.at[k], lab_recv.at[k], device))
    raw_ref[me_col] = sorted_buf[me_col]
    got_label_ref[me_col] = label_ref[me_col]

    def window_sums(w, carry):
        def chunk(i, acc):
            total, square = acc
            values = jnp.log(1.0 + sorted_buf[w, pl.ds(pl.multiple_of(i * step, step), step), :].astype(jnp.float32))
            values = values.reshape(step // 8, 8, values.shape[1])
            return total + jnp.sum(values, axis=0), square + jnp.sum(values * values, axis=0)

        blank = jnp.zeros((8, spectra_ref.shape[2]), jnp.float32)
        total, square = lax.fori_loop(0, frames // step, chunk, (blank, blank))
        sums[w] = jnp.sum(total, axis=0, keepdims=True)
        sums[windows + w] = jnp.sum(square, axis=0, keepdims=True)
        return carry

    lax.fori_loop(0, windows, window_sums, 0)

    def spread(c, carry):
        total = jnp.zeros(part.shape[1:], jnp.float32)
        for w in range(2 * windows):
            total = total + table_ref[c, :, w : w + 1] * sums[w]
        part[c] = total
        return carry

    lax.fori_loop(0, cols, spread, 0)

    first = []
    for k in range(1, cols):
        peer = lax.rem(me_col + k, cols)
        first.append(send(part.at[peer], part_in.at[k], a_send.at[k], a_recv.at[k], (me_row, peer)))
    total = part[me_col]
    for k in range(1, cols):
        first[k - 1].wait_recv()
        total = total + part_in[k]
    share[...] = total
    second = []
    for k in range(1, rows):
        peer = lax.rem(me_row + k, rows)
        second.append(send(share, share_in.at[me_row], b_send.at[k], b_recv.at[k], (peer, me_col)))
    share_in[me_row] = total
    for copy in second:
        copy.wait_recv()
    total = share_in[0]
    for r in range(1, rows):
        total = total + share_in[r]
    stats_ref[me_col] = total
    third = []
    for k in range(1, cols):
        peer = lax.rem(me_col + k, cols)
        third.append(send(stats_ref.at[me_col], stats_ref.at[me_col], c_send.at[k], c_recv.at[k], (me_row, peer)))
    for copy in third + copies:
        copy.wait_recv()
    for copy in first + second + third + copies:
        copy.wait_send()


def exchange(rows, cols, order, spectra, labels, table):
    windows, frames, bins = spectra.shape
    depth = table.shape[1]
    vmem = pl.BlockSpec(memory_space=pltpu.VMEM)
    dma = pltpu.SemaphoreType.DMA
    return pl.pallas_call(
        functools.partial(exchange_kernel, rows, cols),
        out_shape=(
            jax.ShapeDtypeStruct((cols, frames, bins), jnp.bfloat16),
            jax.ShapeDtypeStruct(labels.shape, jnp.int32),
            jax.ShapeDtypeStruct((cols, depth, bins), jnp.float32),
        ),
        in_specs=[pl.BlockSpec(memory_space=pltpu.SMEM), vmem, vmem, vmem],
        out_specs=(vmem, vmem, vmem),
        scratch_shapes=[
            pltpu.VMEM((windows, frames, bins), jnp.bfloat16),
            pltpu.VMEM((2 * windows, 1, bins), jnp.float32),
            pltpu.VMEM((cols, depth, bins), jnp.float32),
            pltpu.VMEM((cols, depth, bins), jnp.float32),
            pltpu.VMEM((depth, bins), jnp.float32),
            pltpu.VMEM((rows, depth, bins), jnp.float32),
        ]
        + [dma((cols,))] * 6 + [dma((rows,))] * 2 + [dma((cols,))] * 2,
        compiler_params=pltpu.CompilerParams(
            collective_id=0, has_side_effects=True, vmem_limit_bytes=48 * 2**20
        ),
    )(order, spectra, labels, table)


class Segment:
    def __init__(self, rows, cols, index, place, src, out, bufs, sems):
        self.rows, self.chips, self.index = rows, cols // 2, index
        self.me_row, self.me_col, self.chip, self.core = place
        self.src, self.out, self.bufs, self.sems = src, out, bufs, sems
        self.open, self.sent = [], []

    def send(self, step, k, src, dst, device):
        send_sem, recv_sem = self.sems[step]
        copy = send(src, dst, send_sem.at[self.index, k], recv_sem.at[self.index, k], device)
        self.open.append(copy)
        self.sent.append(copy)

    def land(self):
        for copy in self.open:
            copy.wait_recv()
        self.open = []

    def step(self, number):
        half_in, quarter, quarter_in, piece, piece_in = (b.at[self.index] for b in self.bufs)
        out, chips, rows = self.out.at[self.index], self.chips, self.rows
        core, chip, me_row = self.core, self.chip, self.me_row
        self.land()
        if number == 0:
            other = 1 - core
            self.send(0, 0, self.src.at[self.index, other], half_in, (me_row, chip * 2 + other))
        elif number == 1:
            def add(q, carry):
                quarter[q] = (self.src[self.index, core, q] + half_in[q]).astype(jnp.bfloat16)
                return carry

            lax.fori_loop(0, chips, add, 0)
            for k in range(1, chips):
                peer = lax.rem(chip + k, chips)
                self.send(1, k, quarter.at[peer], quarter_in.at[k], (me_row, peer * 2 + core))
        elif number == 2:
            def add(r, carry):
                total = self.src[self.index, core, chip, r] + half_in[chip, r]
                for k in range(1, chips):
                    total = total + quarter_in[k, r].astype(jnp.float32)
                piece[r] = total
                return carry

            lax.fori_loop(0, rows, add, 0)
            for k in range(1, rows):
                peer = lax.rem(me_row + k, rows)
                self.send(2, k, piece.at[peer], piece_in.at[k], (peer, self.me_col))
        elif number == 3:
            total = piece[me_row]
            for k in range(1, rows):
                total = total + piece_in[k]
            out[core, chip, me_row] = total.astype(jnp.bfloat16)
            mine = out.at[core, chip, me_row]
            for k in range(1, rows):
                self.send(3, k, mine, mine, (lax.rem(me_row + k, rows), self.me_col))
        elif number == 4:
            mine = out.at[core, chip]
            for k in range(1, chips):
                self.send(4, k, mine, mine, (me_row, lax.rem(chip + k, chips) * 2 + core))
        elif number == 5:
            self.send(5, 0, out.at[core], out.at[core], (me_row, chip * 2 + 1 - core))
        else:
            for copy in self.sent:
                copy.wait_send()


def reduce_kernel(rows, cols, src_ref, out_ref, *scratch):
    me_row, me_col = lax.axis_index("row"), lax.axis_index("col")
    place = (me_row, me_col, me_col // 2, lax.rem(me_col, 2))
    bufs, flat = scratch[:5], scratch[5:]
    sems = [(flat[2 * i], flat[2 * i + 1]) for i in range(6)]
    enter(rows, cols, me_row, me_col)
    segments = [
        Segment(rows, cols, s, place, src_ref, out_ref, bufs, sems) for s in range(SEGMENTS)
    ]
    for time in range(7 + SEGMENTS - 1):
        for s in range(SEGMENTS):
            if 0 <= time - s < 7:
                segments[s].step(time - s)


def reduce_everywhere(rows, cols, stacked):
    chips = cols // 2
    depth = stacked.shape[0] // (SEGMENTS * 2 * chips * rows)
    shape = (SEGMENTS, 2, chips, rows, depth, WIDTH)
    vmem = pl.BlockSpec(memory_space=pltpu.VMEM)
    dma = pltpu.SemaphoreType.DMA
    peers = [1, chips, rows, rows, chips, 1]
    out = pl.pallas_call(
        functools.partial(reduce_kernel, rows, cols),
        out_shape=jax.ShapeDtypeStruct(shape, jnp.bfloat16),
        in_specs=[vmem],
        out_specs=vmem,
        scratch_shapes=[
            pltpu.VMEM((SEGMENTS, chips, rows, depth, WIDTH), jnp.float32),
            pltpu.VMEM((SEGMENTS, chips, rows, depth, WIDTH), jnp.bfloat16),
            pltpu.VMEM((SEGMENTS, chips, rows, depth, WIDTH), jnp.bfloat16),
            pltpu.VMEM((SEGMENTS, rows, depth, WIDTH), jnp.float32),
            pltpu.VMEM((SEGMENTS, rows, depth, WIDTH), jnp.float32),
        ]
        + [dma((SEGMENTS, count)) for count in peers for _ in range(2)],
        compiler_params=pltpu.CompilerParams(
            collective_id=1, has_side_effects=True, vmem_limit_bytes=48 * 2**20
        ),
    )(stacked.reshape(shape))
    return out.reshape(stacked.shape)


def from_rows(value, height):
    return jnp.swapaxes(value.reshape(-1, height, WIDTH), 0, 1).reshape(height, -1)


VFRAMES = 64


def dot(left, right, dims):
    return lax.dot_general(left, right, (dims, ((), ())), preferred_element_type=jnp.float32)


AB = ((1,), (0,))
ABT = ((1,), (1,))
ATB = ((0,), (0,))


def earlier(values):
    row = lax.broadcasted_iota(jnp.int32, values.shape, 0)
    return jnp.where(lax.rem(row, VFRAMES) == 0, 0.0, pltpu.roll(values, 1, 0))


def later(values):
    row = lax.broadcasted_iota(jnp.int32, values.shape, 0)
    return jnp.where(
        lax.rem(row, VFRAMES) == VFRAMES - 1, 0.0, pltpu.roll(values, values.shape[0] - 1, 0)
    )


def logistic(values):
    return 1.0 / (1.0 + jnp.exp(-values))


def silu_slope(values):
    gate = logistic(values)
    return gate * (1.0 + values * (1.0 - gate))


def train_kernel(
    total_windows, id_ref, raw_ref, stats_ref, w1_ref, w2_ref, w3_ref, w4_ref, out_ref,
    plain, xb, db, pre, hat0, hat1, ab, enc2, bb, dec0, dec1, d0, d1, eb, fb, g0, g1,
):
    windows, frames, bins = raw_ref.shape
    rows = windows * VFRAMES
    ch = WIDTH
    block = min(rows, 256)
    per_chunk = stats_ref.shape[1] // 2
    count = WIN_SENSOR * frames
    bf = jnp.bfloat16

    def each_block(body):
        def run(i, carry):
            body(pl.ds(pl.multiple_of(i * block, block), block))
            return carry

        lax.fori_loop(0, rows // block, run, 0)

    def normalize(w, carry):
        sensor = id_ref[w]
        chunk, inner = sensor // per_chunk, lax.rem(sensor, per_chunk)
        center = stats_ref[chunk, pl.ds(inner, 1), :] / count
        square = stats_ref[chunk, pl.ds(per_chunk + inner, 1), :] / count
        factor = lax.rsqrt(square - center * center + EPS)
        for i in range(4):
            part = pl.ds(i * (frames // 4), frames // 4)
            value = (jnp.log(1.0 + raw_ref[w, part, :].astype(jnp.float32)) - center) * factor
            for c in range(4):
                plain[c, part, :] = value[:, c * 128 : (c + 1) * 128]
        at = pl.ds(pl.multiple_of(w * VFRAMES, VFRAMES), VFRAMES)
        for c in range(4):
            quarter = [plain[c, pl.ds(p, VFRAMES, stride=4), :] for p in range(4)]
            six = [earlier(quarter[3])] + quarter + [later(quarter[0])]
            for p in range(6):
                start = p * bins + c * 128
                xb[at, start : start + 128] = six[p].astype(bf)
        return carry

    lax.fori_loop(0, windows, normalize, 0)

    def first_layer(at):
        for q in range(2):
            pre[q, at, :] = dot(xb[at, 1024 * q : 1024 * q + 2048], w1_ref[...], AB)

    each_block(first_layer)
    mean = jnp.sum(pre[0] + pre[1], axis=0, keepdims=True) / (2 * rows)
    spread = jnp.square(pre[0] - mean) + jnp.square(pre[1] - mean)
    inverse = lax.rsqrt(jnp.sum(spread, axis=0, keepdims=True) / (2 * rows) + EPS)

    def forward(at):
        h0 = (pre[0, at, :] - mean) * inverse
        h1 = (pre[1, at, :] - mean) * inverse
        hat0[at, :] = h0
        hat1[at, :] = h1
        a0, a1 = h0 * logistic(h0), h1 * logistic(h1)
        for i, value in enumerate((earlier(a1), a0, a1, later(a0))):
            ab[at, i * ch : (i + 1) * ch] = value.astype(bf)
        e = dot(ab[at, :], w2_ref[...], AB)
        enc2[at, :] = e
        low = (e * logistic(e)).astype(bf)
        bb[at, :] = low
        z = [dot(low, w3_ref[:, i * ch : (i + 1) * ch], AB) for i in range(4)]
        p0, p1 = z[1] + earlier(z[3]), z[2] + later(z[0])
        dec0[at, :] = p0
        dec1[at, :] = p1
        o0, o1 = (p0 * logistic(p0)).astype(bf), (p1 * logistic(p1)).astype(bf)
        d0[at, :] = o0
        d1[at, :] = o1
        for c in range(bins // 256):
            def y(value, i):
                start = i * bins + c * 256
                return dot(value, w4_ref[:, start : start + 256], AB)

            rebuilt = (
                y(o0, 1) + earlier(y(o1, 3)),
                y(o0, 2) + y(o1, 0),
                y(o1, 1) + y(o0, 3),
                y(o1, 2) + later(y(o0, 0)),
            )
            delta = []
            for p in range(4):
                start = (p + 1) * bins + c * 256
                normed = xb[at, start : start + 256].astype(jnp.float32)
                delta.append((rebuilt[p] - normed) / total_windows)
            six = [earlier(delta[3])] + delta + [later(delta[0])]
            for p in range(6):
                start = p * bins + c * 256
                db[at, start : start + 256] = six[p].astype(bf)

    each_block(forward)

    def grad_dec2(i, carry):
        left = pl.ds(pl.multiple_of(i * ch, ch), ch)
        right = pl.ds(pl.multiple_of(2 * bins + i * ch, ch), ch)
        out_ref[left, :] = dot(d0[...], db[:, left], ATB) + dot(d1[...], db[:, right], ATB)
        return carry

    lax.fori_loop(0, 4 * bins // ch, grad_dec2, 0)

    def backward(at):
        e0 = dot(db[at, 0:2048], w4_ref[...], ABT) * silu_slope(dec0[at, :])
        e1 = dot(db[at, 1024:3072], w4_ref[...], ABT) * silu_slope(dec1[at, :])
        for i, value in enumerate((earlier(e1), e0, e1, later(e0))):
            eb[at, i * ch : (i + 1) * ch] = value.astype(bf)
        f = (dot(eb[at, :], w3_ref[...], ABT) * silu_slope(enc2[at, :])).astype(bf)
        fb[at, :] = f
        z = [dot(f, w2_ref[i * ch : (i + 1) * ch, :], ABT) for i in range(4)]
        pre[0, at, :] = (z[1] + earlier(z[3])) * silu_slope(hat0[at, :])
        pre[1, at, :] = (z[2] + later(z[0])) * silu_slope(hat1[at, :])

    each_block(backward)
    base = 4 * bins
    for i in range(4):
        out_ref[base + i * ch : base + (i + 1) * ch, :] = dot(bb[...], eb[:, i * ch : (i + 1) * ch], ATB)
    base += 4 * ch
    for i in range(4):
        out_ref[base + i * ch : base + (i + 1) * ch, :] = dot(ab[:, i * ch : (i + 1) * ch], fb[...], ATB)
    base += 4 * ch
    first = jnp.sum(pre[0] + pre[1], axis=0, keepdims=True) / (2 * rows)
    second = jnp.sum(pre[0] * hat0[...] + pre[1] * hat1[...], axis=0, keepdims=True) / (2 * rows)

    def last(at):
        g0[at, :] = ((pre[0, at, :] - first - hat0[at, :] * second) * inverse).astype(bf)
        g1[at, :] = ((pre[1, at, :] - first - hat1[at, :] * second) * inverse).astype(bf)

    each_block(last)

    def grad_enc1(i, carry):
        left = pl.ds(pl.multiple_of(i * ch, ch), ch)
        right = pl.ds(pl.multiple_of(2 * bins + i * ch, ch), ch)
        to = pl.ds(pl.multiple_of(base + i * ch, ch), ch)
        out_ref[to, :] = dot(xb[:, left], g0[...], ATB) + dot(xb[:, right], g1[...], ATB)
        return carry

    lax.fori_loop(0, 4 * bins // ch, grad_enc1, 0)


def train(total_windows, ids, raw, stats, w_enc1, w_enc2, w_dec1, w_dec2):
    windows, frames, bins = raw.shape
    rows = windows * VFRAMES
    vmem = pl.BlockSpec(memory_space=pltpu.VMEM)

    def wide(columns):
        return pltpu.VMEM((rows, columns), jnp.bfloat16)

    def full(columns):
        return pltpu.VMEM((rows, columns), jnp.float32)

    return pl.pallas_call(
        functools.partial(train_kernel, total_windows),
        out_shape=jax.ShapeDtypeStruct((8 * bins + 8 * WIDTH, WIDTH), jnp.float32),
        in_specs=[pl.BlockSpec(memory_space=pltpu.SMEM)] + [vmem] * 6,
        out_specs=vmem,
        scratch_shapes=[
            pltpu.VMEM((4, frames, 128), jnp.float32),
            wide(6 * bins),
            wide(6 * bins),
            pltpu.VMEM((2, rows, WIDTH), jnp.float32),
            full(WIDTH), full(WIDTH),
            wide(4 * WIDTH),
            full(WIDTH),
            wide(WIDTH),
            full(WIDTH), full(WIDTH),
            wide(WIDTH), wide(WIDTH),
            wide(4 * WIDTH),
            wide(WIDTH), wide(WIDTH), wide(WIDTH),
        ],
        compiler_params=pltpu.CompilerParams(vmem_limit_bytes=56 * 2**20),
    )(ids, raw, stats, w_enc1, w_enc2, w_dec1, w_dec2)


def sensor_table(sensor_col, sensor_total):
    return (sensor_col[:, None] == jnp.arange(sensor_total, dtype=jnp.int32)[None, :]).astype(
        jnp.float32
    )


def local(spectra, sensor_ids, permutation, w_enc1, w_enc2, w_dec1, w_dec2):
    window_count = spectra.shape[0]
    frame_count = spectra.shape[1]
    row_count = lax.axis_size("row")
    col_count = lax.axis_size("col")
    total_windows = window_count * row_count * col_count
    sensor_total = total_windows // WIN_SENSOR
    per_row = col_count // row_count
    sensor_col = sensor_ids[:, 0]
    trainer = permutation // window_count
    target = trainer // col_count * per_row + trainer % per_row
    slots = jnp.arange(window_count, dtype=jnp.int32)
    order = jnp.sum(jnp.where(target[None, :] == slots[:, None], slots[None, :], 0), axis=1)
    owner = jnp.sum(
        jnp.where(target[None, :] == slots[:, None], sensor_col[None, :], 0), axis=1
    )
    per_chunk = sensor_total // col_count
    table = sensor_table(owner, sensor_total).T.reshape(col_count, per_chunk, window_count)
    blank = jnp.zeros_like(table)
    table = jnp.concatenate(
        [
            jnp.concatenate([table, blank], axis=2),
            jnp.concatenate([blank, table], axis=2),
        ],
        axis=1,
    )
    labels = jnp.broadcast_to(owner[:, None, None], (window_count, 8, 128))
    raw, labels, stats = exchange(row_count, col_count, order, spectra, labels, table)
    stacked = train(
        total_windows, labels[:, 0, 0], raw, stats, w_enc1, w_enc2, w_dec1, w_dec2
    )
    stacked = reduce_everywhere(row_count, col_count, stacked).astype(jnp.float32)
    grads, start = [], 0
    for weight in (w_dec2, w_dec1, w_enc2, w_enc1):
        stop = start + weight.size // WIDTH
        grads.append(from_rows(stacked[start:stop], weight.shape[0]))
        start = stop
    return tuple(grads[::-1])


def solution(mesh):
    return jax.shard_map(
        local,
        mesh=mesh,
        in_specs=(
            P(("row", "col"), None, None),
            P(("row", "col"), None),
            P(("row", "col")),
            P(),
            P(),
            P(),
            P(),
        ),
        out_specs=(P(), P(), P(), P()),
        check_vma=False,
    )
```

profile of v0, /device:TPU:0, one launch (start us, length us, event | category | flops | bytes accessed | tf_op | source)
XLA Modules:
  0.0 130.4 jit_solution(7169504409343931304)
XLA Ops:
  0.6 0.7 fusion
  1.3 0.8 select_reduce_fusion
  2.1 0.1 compare_convert_fusion
  2.2 0.1 select_maximum_fusion.table_ref
  2.3 0.1 broadcast_in_dim.38.label_ref
  2.4 0.0 copy-start
  2.4 1.6 %copy-done = bf16[8,256,512]{2,1,0:T(8,128)(2,1)S(1)} copy-done((bf16[8,256,512]{2,1,0:T(8,128)(2,1)S(1)}, bf16[8,256,512]{2,1,0:T(8,128)(2,1)}, u32[]{:S(2)}) %copy-start) | copy-done | bytes 2097176
  4.0 40.3 %shard_map.102 = (bf16[8,256,512]{2,1,0:T(8,128)(2,1)S(1)}, s32[8,8,128]{2,1,0:T(8,128)S(1)}, f32[8,8,512]{2,1,0:T(8,128)S(1)}) custom-call(s32[8]{0:T(128)S(1)} %get-tuple-element.11.order_ref, bf16[8,256,512]{2,1,0:T(8,128)(2,1)S(1)} %copy-done, s32[8,8,128]{2,1,0:T(8,128)S(1)} %broadcast_in_dim.38.label_ref, f32[8,8,16]{2,1,0:T(8,128)S(1)} %select_maximum_fusion.table_ref), custom_call_target="tpu_custom_call" | custom-call | tf_op jit(solution)/shard_map/pallas_call | solution.py:125
  44.3 0.0 copy-start.1
  44.3 1.3 %copy-done.1 = bf16[8,256,512]{2,1,0:T(8,128)(2,1)} copy-done((bf16[8,256,512]{2,1,0:T(8,128)(2,1)}, bf16[8,256,512]{2,1,0:T(8,128)(2,1)S(1)}, u32[]{:S(2)}) %copy-start.1) | copy-done | bytes 2097176
  45.6 0.0 copy-start.2
  45.6 0.7 copy-done.2
  46.3 0.8 slice_reduce_fusion.id_ref
  47.0 21.4 %shard_map.103 = f32[6144,256]{1,0:T(8,128)} custom-call(s32[8]{0:T(128)} %slice_reduce_fusion.id_ref, bf16[8,256,512]{2,1,0:T(8,128)(2,1)} %copy-done.1, f32[8,8,512]{2,1,0:T(8,128)} %copy-done.2, bf16[2048,256]{1,0:T(8,128)(2,1)} %w1_ref.1, bf16[1024,256]{1,0:T(8,128)(2,1)} %w2_ref.1, bf16[256,1024]{1,0:T(8,128)(2,1)} %w3_ref.1, bf16[256,2048]{1,0:T(8,128)(2,1)} %w4_ref.1), custom_call_target="tpu_custom_call" | custom-call | tf_op jit(solution)/shard_map/pallas_call | solution.py:443
  68.4 54.9 %shard_map.104 = bf16[3,2,4,4,64,256]{5,4,3,2,1,0:T(8,128)(2,1)S(1)} custom-call(f32[3,2,4,4,64,256]{5,4,3,2,1,0:T(8,128)} %bitcast.13), custom_call_target="tpu_custom_call" | custom-call | tf_op jit(solution)/shard_map/pallas_call | solution.py:237
  123.3 0.9 convert_element_type.12
  124.2 1.1 fusion.1
  125.3 0.7 copy.15
  126.0 1.2 copy.18
  127.1 1.7 %fusion.2 = (f32[1,2,4,4,64,256]{5,4,3,2,1,0:T(8,128)S(1)}, f32[1,2,4,4,64,256]{5,4,3,2,1,0:T(8,128)}) fusion(bf16[3,2,4,4,64,256]{5,4,3,2,1,0:T(8,128)(2,1)S(1)} %shard_map.104), kind=kLoop, calls=%fused_computation.21 | loop fusion | bytes 8388608 | tf_op jit(solution)/shard_map/slice | solution.py:507
  128.8 1.6 %copy.17 = f32[8,32,8,256]{3,2,0,1:T(8,128)} copy(f32[8,32,8,256]{3,2,1,0:T(8,128)S(1)} %bitcast.15) | data formatting | bytes 4194304 | tf_op jit(solution)/shard_map/reshape | solution.py:258
  (1 shorter events, 0.0 us)
Async XLA Ops:
  2.4 1.6 %copy-start = (bf16[8,256,512]{2,1,0:T(8,128)(2,1)S(1)}, bf16[8,256,512]{2,1,0:T(8,128)(2,1)}, u32[]{:S(2)}) copy-start(bf16[8,256,512]{2,1,0:T(8,128)(2,1)} %spectra_ref.1) | copy-start | bytes 6291460
  44.3 1.3 %copy-start.1 = (bf16[8,256,512]{2,1,0:T(8,128)(2,1)}, bf16[8,256,512]{2,1,0:T(8,128)(2,1)S(1)}, u32[]{:S(2)}) copy-start(bf16[8,256,512]{2,1,0:T(8,128)(2,1)S(1)} %get-tuple-element.8.raw_ref) | copy-start | bytes 6291460
  45.6 0.7 copy-start.2
where the time goes:
time: 131 us; the launch traced here: 130 us
  Pallas kernels  117 us (89%)
  local copies, waits for them, and re-layouts  10.6 us (8%)
  other arithmetic  2.52 us (2%)
    pallas_call x1, Pallas kernels, reduce_everywhere(): pl.pallas_call(functools.partial(reduce_kernel, rows, cols), out_shape=ja...  54.9 us
    pallas_call x1, Pallas kernels, exchange(): pl.pallas_call(functools.partial(exchange_kernel, rows, cols), out_shape=...  40.3 us
    pallas_call x1, Pallas kernels, train(): pl.pallas_call(functools.partial(train_kernel, total_windows), out_shape=...  21.4 us
    unnamed x7, local copies, waits for them, and re-layouts  4.73 us
    slice x2, local copies, waits for them, and re-layouts, local(): grads.append(from_rows(stacked[start:stop], weight.shape[0]))  2.82 us

commit v1 on v0

--- a/solution.py
+++ b/solution.py
@@ -12,7 +12,6 @@
 
 EPS = 1e-05
 MESH = pl.DeviceIdType.MESH
-SEGMENTS = 3
 WIDTH = 256
 
 
@@ -55,10 +54,22 @@
         sorted_buf[w] = spectra_ref[order_ref[w]]
     enter(rows, cols, me_row, me_col)
     copies = []
+
+    def batch(number, start, size):
+        part = pl.ds(start, size)
+        for k in range(1, cols):
+            peer = lax.rem(me_col + k, cols)
+            copies.append(
+                send(
+                    sorted_buf.at[peer, part], raw_ref.at[me_col, part],
+                    raw_send.at[number, k], raw_recv.at[number, k], (me_row, peer),
+                )
+            )
+
+    batch(0, 0, frames // 2)
     for k in range(1, cols):
         peer = lax.rem(me_col + k, cols)
         device = (me_row, peer)
-        copies.append(send(sorted_buf.at[peer], raw_ref.at[me_col], raw_send.at[k], raw_recv.at[k], device))
         copies.append(send(label_ref.at[peer], got_label_ref.at[me_col], lab_send.at[k], lab_recv.at[k], device))
     raw_ref[me_col] = sorted_buf[me_col]
     got_label_ref[me_col] = label_ref[me_col]
@@ -91,6 +102,7 @@
     for k in range(1, cols):
         peer = lax.rem(me_col + k, cols)
         first.append(send(part.at[peer], part_in.at[k], a_send.at[k], a_recv.at[k], (me_row, peer)))
+    batch(1, frames // 2, frames // 4)
     total = part[me_col]
     for k in range(1, cols):
         first[k - 1].wait_recv()
@@ -111,6 +123,7 @@
     for k in range(1, cols):
         peer = lax.rem(me_col + k, cols)
         third.append(send(stats_ref.at[me_col], stats_ref.at[me_col], c_send.at[k], c_recv.at[k], (me_row, peer)))
+    batch(2, frames // 2 + frames // 4, frames // 4)
     for copy in third + copies:
         copy.wait_recv()
     for copy in first + second + third + copies:
@@ -139,7 +152,7 @@
             pltpu.VMEM((depth, bins), jnp.float32),
             pltpu.VMEM((rows, depth, bins), jnp.float32),
         ]
-        + [dma((cols,))] * 6 + [dma((rows,))] * 2 + [dma((cols,))] * 2,
+        + [dma((3, cols))] * 2 + [dma((cols,))] * 4 + [dma((rows,))] * 2 + [dma((cols,))] * 2,
         compiler_params=pltpu.CompilerParams(
             collective_id=0, has_side_effects=True, vmem_limit_bytes=48 * 2**20
         ),
@@ -218,19 +231,27 @@
     bufs, flat = scratch[:5], scratch[5:]
     sems = [(flat[2 * i], flat[2 * i + 1]) for i in range(6)]
     enter(rows, cols, me_row, me_col)
+    count = src_ref.shape[0]
     segments = [
-        Segment(rows, cols, s, place, src_ref, out_ref, bufs, sems) for s in range(SEGMENTS)
+        Segment(rows, cols, s, place, src_ref, out_ref, bufs, sems) for s in range(count)
     ]
-    for time in range(7 + SEGMENTS - 1):
-        for s in range(SEGMENTS):
-            if 0 <= time - s < 7:
-                segments[s].step(time - s)
+    for number in range(2):
+        for segment in segments:
+            segment.step(number)
+    for time in range(4 + count):
+        for s in range(count):
+            if 0 <= time - s < 4:
+                segments[s].step(2 + time - s)
+    for segment in segments:
+        segment.step(6)
 
 
 def reduce_everywhere(rows, cols, stacked):
     chips = cols // 2
-    depth = stacked.shape[0] // (SEGMENTS * 2 * chips * rows)
-    shape = (SEGMENTS, 2, chips, rows, depth, WIDTH)
+    unit = 16 * 2 * chips * rows
+    segments = 6 if stacked.shape[0] % (6 * unit) == 0 else 3
+    depth = stacked.shape[0] // (segments * 2 * chips * rows)
+    shape = (segments, 2, chips, rows, depth, WIDTH)
     vmem = pl.BlockSpec(memory_space=pltpu.VMEM)
     dma = pltpu.SemaphoreType.DMA
     peers = [1, chips, rows, rows, chips, 1]
@@ -240,13 +261,13 @@
         in_specs=[vmem],
         out_specs=vmem,
         scratch_shapes=[
-            pltpu.VMEM((SEGMENTS, chips, rows, depth, WIDTH), jnp.float32),
-            pltpu.VMEM((SEGMENTS, chips, rows, depth, WIDTH), jnp.bfloat16),
-            pltpu.VMEM((SEGMENTS, chips, rows, depth, WIDTH), jnp.bfloat16),
-            pltpu.VMEM((SEGMENTS, rows, depth, WIDTH), jnp.float32),
-            pltpu.VMEM((SEGMENTS, rows, depth, WIDTH), jnp.float32),
+            pltpu.VMEM((segments, chips, rows, depth, WIDTH), jnp.float32),
+            pltpu.VMEM((segments, chips, rows, depth, WIDTH), jnp.bfloat16),
+            pltpu.VMEM((segments, chips, rows, depth, WIDTH), jnp.bfloat16),
+            pltpu.VMEM((segments, rows, depth, WIDTH), jnp.float32),
+            pltpu.VMEM((segments, rows, depth, WIDTH), jnp.float32),
         ]
-        + [dma((SEGMENTS, count)) for count in peers for _ in range(2)],
+        + [dma((segments, count)) for count in peers for _ in range(2)],
         compiler_params=pltpu.CompilerParams(
             collective_id=1, has_side_effects=True, vmem_limit_bytes=48 * 2**20
         ),
@@ -254,8 +275,26 @@
     return out.reshape(stacked.shape)
 
 
-def from_rows(value, height):
-    return jnp.swapaxes(value.reshape(-1, height, WIDTH), 0, 1).reshape(height, -1)
+def unstack_kernel(stacked_ref, *out_refs):
+    start = 0
+    for out in out_refs:
+        height = out.shape[0]
+        for c in range(out.shape[1] // WIDTH):
+            for i in range(0, height, 256):
+                piece = stacked_ref[start + i : start + i + 256, :].astype(jnp.float32)
+                out[i : i + 256, c * WIDTH : (c + 1) * WIDTH] = piece
+            start += height
+
+
+def unstack(stacked, shapes):
+    vmem = pl.BlockSpec(memory_space=pltpu.VMEM)
+    return pl.pallas_call(
+        unstack_kernel,
+        out_shape=tuple(jax.ShapeDtypeStruct(shape, jnp.float32) for shape in shapes),
+        in_specs=[vmem],
+        out_specs=(vmem,) * len(shapes),
+        compiler_params=pltpu.CompilerParams(vmem_limit_bytes=24 * 2**20),
+    )(stacked)
 
 
 VFRAMES = 64
@@ -459,7 +498,7 @@
             wide(4 * WIDTH),
             wide(WIDTH), wide(WIDTH), wide(WIDTH),
         ],
-        compiler_params=pltpu.CompilerParams(vmem_limit_bytes=56 * 2**20),
+        compiler_params=pltpu.CompilerParams(vmem_limit_bytes=(40 if windows <= 8 else 56) * 2**20),
     )(ids, raw, stats, w_enc1, w_enc2, w_dec1, w_dec2)
 
 
@@ -500,12 +539,8 @@
     stacked = train(
         total_windows, labels[:, 0, 0], raw, stats, w_enc1, w_enc2, w_dec1, w_dec2
     )
-    stacked = reduce_everywhere(row_count, col_count, stacked).astype(jnp.float32)
-    grads, start = [], 0
-    for weight in (w_dec2, w_dec1, w_enc2, w_enc1):
-        stop = start + weight.size // WIDTH
-        grads.append(from_rows(stacked[start:stop], weight.shape[0]))
-        start = stop
+    stacked = reduce_everywhere(row_count, col_count, stacked)
+    grads = unstack(stacked, [w.shape for w in (w_dec2, w_dec1, w_enc2, w_enc1)])
     return tuple(grads[::-1])
 
 

time: 131 us -> 121 us (0.924)
  Pallas kernels: 117 us -> 112 us
  local copies, waits for them, and re-layouts: 10.6 us -> 6.64 us
    pallas_call x1, Pallas kernels: 40.3 us -> 34 us  [exchange(): pl.pallas_call(functools.partial(exchange_kernel, rows, cols), out_shape=...]
    pallas_call x1, Pallas kernels: 21.4 us -> 16.8 us  [train(): pl.pallas_call(functools.partial(train_kernel, total_windows), out_shape=...]
    pallas_call x1, Pallas kernels: 54.9 us -> 58 us  [reduce_everywhere(): pl.pallas_call(functools.partial(reduce_kernel, rows, cols), out_shape=ja...]
    pallas_call x0 -> x1, Pallas kernels: none -> 2.97 us  [unstack(): pl.pallas_call(unstack_kernel, out_shape=tuple((jax.ShapeDtypeStruct(shap...]
    slice x2 -> x0, local copies, waits for them, and re-layouts: 2.82 us -> none  [local(): grads.append(from_rows(stacked[start:stop], weight.shape[0]))]
    reshape x2 -> x0, local copies, waits for them, and re-layouts: 2.28 us -> none  [the longest x1 1.6 us: from_rows(): jnp.swapaxes(value.reshape(-1, height, WIDTH), 0, 1).reshape(height, -1)]
    unnamed x7 -> x12, local copies, waits for them, and re-layouts: 4.73 us -> 6.33 us
where the time goes in v1:
time: 121 us
  Pallas kernels  112 us (93%)
  local copies, waits for them, and re-layouts  6.64 us (5%)
  other arithmetic  1.64 us (1%)
    pallas_call x1, Pallas kernels, reduce_everywhere(): pl.pallas_call(functools.partial(reduce_kernel, rows, cols), out_shape=ja...  58 us
    pallas_call x1, Pallas kernels, exchange(): pl.pallas_call(functools.partial(exchange_kernel, rows, cols), out_shape=...  34 us
    pallas_call x1, Pallas kernels, train(): pl.pallas_call(functools.partial(train_kernel, total_windows), out_shape=...  16.8 us
    unnamed x12, local copies, waits for them, and re-layouts  6.33 us
    pallas_call x1, Pallas kernels, unstack(): pl.pallas_call(unstack_kernel, out_shape=tuple((jax.ShapeDtypeStruct(shap...  2.97 us

profile of v1, /device:TPU:0, one launch (start us, length us, event | category | flops | bytes accessed | tf_op | source)
XLA Modules:
  0.0 120.8 jit_solution(161863790683660371)
XLA Ops:
  0.6 0.7 fusion
  1.3 0.8 select_reduce_fusion
  2.1 0.1 compare_convert_fusion
  2.2 0.1 select_maximum_fusion.table_ref
  2.3 0.1 broadcast_in_dim.38.label_ref
  2.4 0.0 copy-start.1
  2.4 1.6 %copy-done.1 = bf16[8,256,512]{2,1,0:T(8,128)(2,1)S(1)} copy-done((bf16[8,256,512]{2,1,0:T(8,128)(2,1)S(1)}, bf16[8,256,512]{2,1,0:T(8,128)(2,1)}, u32[]{:S(2)}) %copy-start.1) | copy-done | bytes 2097176
  4.0 0.0 copy-start.2
  4.0 0.0 copy-start.3
  4.0 34.0 %shard_map.102 = (bf16[8,256,512]{2,1,0:T(8,128)(2,1)S(1)}, s32[8,8,128]{2,1,0:T(8,128)S(1)}, f32[8,8,512]{2,1,0:T(8,128)S(1)}) custom-call(s32[8]{0:T(128)S(1)} %get-tuple-element.19.order_ref, bf16[8,256,512]{2,1,0:T(8,128)(2,1)S(1)} %copy-done.1, s32[8,8,128]{2,1,0:T(8,128)S(1)} %broadcast_in_dim.38.label_ref, f32[8,8,16]{2,1,0:T(8,128)S(1)} %select_maximum_fusion.table_ref), custom_call_target="tpu_custom_call" | custom-call | tf_op jit(solution)/shard_map/pallas_call | solution.py:138
  38.0 0.2 slice_reduce_fusion.id_ref
  38.2 0.0 copy-done.2
  38.2 0.0 copy-done.3
  38.2 0.0 copy-start.4
  38.2 1.0 copy-done.4
  39.3 0.0 copy-start.5
  39.3 1.0 copy-done.5
  40.3 16.8 %shard_map.103 = f32[6144,256]{1,0:T(8,128)S(1)} custom-call(s32[8]{0:T(128)S(1)} %slice_reduce_fusion.id_ref, bf16[8,256,512]{2,1,0:T(8,128)(2,1)S(1)} %get-tuple-element.12.raw_ref, f32[8,8,512]{2,1,0:T(8,128)S(1)} %get-tuple-element.13.stats_ref, bf16[2048,256]{1,0:T(8,128)(2,1)S(1)} %copy-done.2, bf16[1024,256]{1,0:T(8,128)(2,1)S(1)} %copy-done.4, ...), custom_call_target="tpu_custom_call" | custom-call | tf_op jit(solution)/shard_map/pallas_call | solution.py:482
  57.1 0.0 copy-start
  57.1 2.6 %copy-done = f32[6144,256]{1,0:T(8,128)} copy-done((f32[6144,256]{1,0:T(8,128)}, f32[6144,256]{1,0:T(8,128)S(1)}, u32[]{:S(2)}) %copy-start) | copy-done | bytes 6291480
  59.8 58.0 %shard_map.104 = bf16[6,2,4,4,32,256]{5,4,3,2,1,0:T(8,128)(2,1)S(1)} custom-call(f32[6,2,4,4,32,256]{5,4,3,2,1,0:T(8,128)} %bitcast.3), custom_call_target="tpu_custom_call" | custom-call | tf_op jit(solution)/shard_map/pallas_call | solution.py:258
  117.8 3.0 %shard_map.105 = (f32[256,2048]{1,0:T(8,128)}, f32[256,1024]{1,0:T(8,128)}, f32[1024,256]{1,0:T(8,128)}, f32[2048,256]{1,0:T(8,128)}) custom-call(bf16[6144,256]{1,0:T(8,128)(2,1)S(1)} %bitcast.4), custom_call_target="tpu_custom_call" | custom-call | tf_op jit(solution)/shard_map/pallas_call | solution.py:291
  (1 shorter events, 0.0 us)
Async XLA Ops:
  2.4 1.6 %copy-start.1 = (bf16[8,256,512]{2,1,0:T(8,128)(2,1)S(1)}, bf16[8,256,512]{2,1,0:T(8,128)(2,1)}, u32[]{:S(2)}) copy-start(bf16[8,256,512]{2,1,0:T(8,128)(2,1)} %spectra_ref.1) | copy-start | bytes 6291460
  4.0 34.2 %copy-start.2 = (bf16[2048,256]{1,0:T(8,128)(2,1)S(1)}, bf16[2048,256]{1,0:T(8,128)(2,1)}, u32[]{:S(2)}) copy-start(bf16[2048,256]{1,0:T(8,128)(2,1)} %w1_ref.1) | copy-start | bytes 3145732
  4.0 34.3 %copy-start.3 = (bf16[256,2048]{1,0:T(8,128)(2,1)S(1)}, bf16[256,2048]{1,0:T(8,128)(2,1)}, u32[]{:S(2)}) copy-start(bf16[256,2048]{1,0:T(8,128)(2,1)} %w4_ref.1) | copy-start | bytes 3145732
  38.2 1.0 copy-start.4
  39.3 1.0 copy-start.5
  57.1 2.7 %copy-start = (f32[6144,256]{1,0:T(8,128)}, f32[6144,256]{1,0:T(8,128)S(1)}, u32[]{:S(2)}) copy-start(f32[6144,256]{1,0:T(8,128)S(1)} %shard_map.103) | copy-start | bytes 18874372

commit v2 on v1

--- a/solution.py
+++ b/solution.py
@@ -102,7 +102,7 @@
     for k in range(1, cols):
         peer = lax.rem(me_col + k, cols)
         first.append(send(part.at[peer], part_in.at[k], a_send.at[k], a_recv.at[k], (me_row, peer)))
-    batch(1, frames // 2, frames // 4)
+    batch(1, frames // 2, frames * 3 // 8)
     total = part[me_col]
     for k in range(1, cols):
         first[k - 1].wait_recv()
@@ -123,7 +123,7 @@
     for k in range(1, cols):
         peer = lax.rem(me_col + k, cols)
         third.append(send(stats_ref.at[me_col], stats_ref.at[me_col], c_send.at[k], c_recv.at[k], (me_row, peer)))
-    batch(2, frames // 2 + frames // 4, frames // 4)
+    batch(2, frames * 7 // 8, frames // 8)
     for copy in third + copies:
         copy.wait_recv()
     for copy in first + second + third + copies:

time: 121 us -> 121 us (level)
  no operation moved by 1% of the time
where the time goes in v2:
time: 121 us; the launch traced here: 120 us
  Pallas kernels  111 us (92%)
  local copies, waits for them, and re-layouts  6.64 us (5%)
  other arithmetic  1.64 us (1%)
    pallas_call x1, Pallas kernels, reduce_everywhere(): pl.pallas_call(functools.partial(reduce_kernel, rows, cols), out_shape=ja...  57.5 us
    pallas_call x1, Pallas kernels, exchange(): pl.pallas_call(functools.partial(exchange_kernel, rows, cols), out_shape=...  34.3 us
    pallas_call x1, Pallas kernels, train(): pl.pallas_call(functools.partial(train_kernel, total_windows), out_shape=...  16.8 us
    unnamed x12, local copies, waits for them, and re-layouts  6.33 us
    pallas_call x1, Pallas kernels, unstack(): pl.pallas_call(unstack_kernel, out_shape=tuple((jax.ShapeDtypeStruct(shap...  2.97 us

profile of v2, /device:TPU:0, one launch (start us, length us, event | category | flops | bytes accessed | tf_op | source)
XLA Modules:
  0.0 120.4 jit_solution(16560116908520000291)
XLA Ops:
  0.6 0.7 fusion
  1.3 0.8 select_reduce_fusion
  2.1 0.1 compare_convert_fusion
  2.2 0.1 select_maximum_fusion.table_ref
  2.3 0.1 broadcast_in_dim.38.label_ref
  2.4 0.0 copy-start.1
  2.4 1.6 %copy-done.1 = bf16[8,256,512]{2,1,0:T(8,128)(2,1)S(1)} copy-done((bf16[8,256,512]{2,1,0:T(8,128)(2,1)S(1)}, bf16[8,256,512]{2,1,0:T(8,128)(2,1)}, u32[]{:S(2)}) %copy-start.1) | copy-done | bytes 2097176
  4.0 0.0 copy-start.2
  4.0 0.0 copy-start.3
  4.0 34.3 %shard_map.102 = (bf16[8,256,512]{2,1,0:T(8,128)(2,1)S(1)}, s32[8,8,128]{2,1,0:T(8,128)S(1)}, f32[8,8,512]{2,1,0:T(8,128)S(1)}) custom-call(s32[8]{0:T(128)S(1)} %get-tuple-element.19.order_ref, bf16[8,256,512]{2,1,0:T(8,128)(2,1)S(1)} %copy-done.1, s32[8,8,128]{2,1,0:T(8,128)S(1)} %broadcast_in_dim.38.label_ref, f32[8,8,16]{2,1,0:T(8,128)S(1)} %select_maximum_fusion.table_ref), custom_call_target="tpu_custom_call" | custom-call | tf_op jit(solution)/shard_map/pallas_call | solution.py:138
  38.2 0.2 slice_reduce_fusion.id_ref
  38.5 0.0 copy-done.2
  38.5 0.0 copy-done.3
  38.5 0.0 copy-start.4
  38.5 1.0 copy-done.4
  39.5 0.0 copy-start.5
  39.5 1.0 copy-done.5
  40.6 16.8 %shard_map.103 = f32[6144,256]{1,0:T(8,128)S(1)} custom-call(s32[8]{0:T(128)S(1)} %slice_reduce_fusion.id_ref, bf16[8,256,512]{2,1,0:T(8,128)(2,1)S(1)} %get-tuple-element.12.raw_ref, f32[8,8,512]{2,1,0:T(8,128)S(1)} %get-tuple-element.13.stats_ref, bf16[2048,256]{1,0:T(8,128)(2,1)S(1)} %copy-done.2, bf16[1024,256]{1,0:T(8,128)(2,1)S(1)} %copy-done.4, ...), custom_call_target="tpu_custom_call" | custom-call | tf_op jit(solution)/shard_map/pallas_call | solution.py:482
  57.3 0.0 copy-start
  57.4 2.6 %copy-done = f32[6144,256]{1,0:T(8,128)} copy-done((f32[6144,256]{1,0:T(8,128)}, f32[6144,256]{1,0:T(8,128)S(1)}, u32[]{:S(2)}) %copy-start) | copy-done | bytes 6291480
  60.0 57.5 %shard_map.104 = bf16[6,2,4,4,32,256]{5,4,3,2,1,0:T(8,128)(2,1)S(1)} custom-call(f32[6,2,4,4,32,256]{5,4,3,2,1,0:T(8,128)} %bitcast.3), custom_call_target="tpu_custom_call" | custom-call | tf_op jit(solution)/shard_map/pallas_call | solution.py:258
  117.5 3.0 %shard_map.105 = (f32[256,2048]{1,0:T(8,128)}, f32[256,1024]{1,0:T(8,128)}, f32[1024,256]{1,0:T(8,128)}, f32[2048,256]{1,0:T(8,128)}) custom-call(bf16[6144,256]{1,0:T(8,128)(2,1)S(1)} %bitcast.4), custom_call_target="tpu_custom_call" | custom-call | tf_op jit(solution)/shard_map/pallas_call | solution.py:291
  (1 shorter events, 0.0 us)
Async XLA Ops:
  2.4 1.6 %copy-start.1 = (bf16[8,256,512]{2,1,0:T(8,128)(2,1)S(1)}, bf16[8,256,512]{2,1,0:T(8,128)(2,1)}, u32[]{:S(2)}) copy-start(bf16[8,256,512]{2,1,0:T(8,128)(2,1)} %spectra_ref.1) | copy-start | bytes 6291460
  4.0 34.5 %copy-start.2 = (bf16[2048,256]{1,0:T(8,128)(2,1)S(1)}, bf16[2048,256]{1,0:T(8,128)(2,1)}, u32[]{:S(2)}) copy-start(bf16[2048,256]{1,0:T(8,128)(2,1)} %w1_ref.1) | copy-start | bytes 3145732
  4.0 34.5 %copy-start.3 = (bf16[256,2048]{1,0:T(8,128)(2,1)S(1)}, bf16[256,2048]{1,0:T(8,128)(2,1)}, u32[]{:S(2)}) copy-start(bf16[256,2048]{1,0:T(8,128)(2,1)} %w4_ref.1) | copy-start | bytes 3145732
  38.5 1.0 copy-start.4
  39.5 1.0 copy-start.5
  57.3 2.7 %copy-start = (f32[6144,256]{1,0:T(8,128)}, f32[6144,256]{1,0:T(8,128)S(1)}, u32[]{:S(2)}) copy-start(f32[6144,256]{1,0:T(8,128)S(1)} %shard_map.103) | copy-start | bytes 18874372
